TPU v7x, 256 devices: a whole 4x4x8 slice. The times are simulated.
256 devices in a mesh: tm: 32 (over x, z), rows: 8 (over y, core).
Axes of the slice: x: 4, y: 4, z: 8, core: 2. Of those that a mesh axis runs over, the one named last changes fastest.
Arguments:
- queries: bfloat16 [64, 16, 80, 2240], P('tm', 'rows'), may hold values from -8 to 8
- key_rows: bfloat16 [64, 16, 80, 2240], P('tm', 'rows'), may hold values from -8 to 8
- value_rows: bfloat16 [64, 16, 80, 2240], P('tm', 'rows'), may hold values from -8 to 8
- hidden: bfloat16 [64, 16, 80, 5600], P('tm', 'rows'), may hold values from -6 to 6
- conv_weight: float32 [3, 3, 5600], replicated, may hold values from -2 to 2
- conv_bias: float32 [5600], replicated, may hold values from -2 to 2
Outputs:
- attended: float32 [64, 16, 80, 2240], P('tm', 'rows')
- gated: bfloat16 [64, 16, 80, 2800], P('tm', 'rows')
All inputs are finite; a program needn't handle non-finite values.
Results may differ from a plain program's by a relative error of at most 0.0029.
Values may be sent and summed in bfloat16 or wider, within the bound.
A program may use at most 320 MiB of HBM per device.

v0:
```python
import jax
import jax.numpy as jnp
from jax import lax
from jax.sharding import PartitionSpec as P

HEADS = 20
HDIM = 112


def prefix(value, axis, combine, identity):
    length, place = (lax.axis_size(axis), lax.axis_index(axis))
    everything = jax.tree.map(
        lambda part, kind: lax.all_gather(part.astype(kind), axis),
        value,
        (jnp.bfloat16, jnp.bfloat16),
    )
    start = jax.tree.map(
        lambda part, zero: jnp.broadcast_to(jnp.asarray(zero, part.dtype), part.shape),
        value,
        identity,
    )

    def lap(k, before):
        reached = k < place
        new = combine(
            before, jax.tree.map(lambda part, own: part[k].astype(own.dtype), everything, value)
        )
        return jax.tree.map(lambda a, b: jnp.where(reached, a, b), new, before)

    return lax.fori_loop(0, length, lap, start)


def padded_2(block, sides, width):
    for axis, dim in sides:
        count = lax.axis_size(axis)
        forward = [(i, i + 1) for i in range(count - 1)]
        backward = [(target, source) for source, target in forward]
        low = lax.ppermute(
            lax.slice_in_dim(block, block.shape[dim] - width, None, axis=dim), axis, forward
        )
        high = lax.ppermute(lax.slice_in_dim(block, 0, width, axis=dim), axis, backward)
        block = jnp.concatenate([low, block, high], axis=dim)
    return block


def features(block):
    return (jax.nn.elu(block.astype(jnp.float32)) + 1.0).astype(jnp.bfloat16)


def add_pair(earlier, later):
    return (earlier[0] + later[0], earlier[1] + later[1])


def on_device(queries, key_rows, value_rows, hidden, conv_weight, conv_bias):
    frame_count, row_count, col_count, width = queries.shape
    shape = (frame_count, row_count * col_count, HEADS, HDIM)
    phi_query = features(queries).reshape(shape)
    phi_key = features(key_rows).reshape(shape)
    value_heads = value_rows.reshape(shape)
    state_part = jnp.einsum(
        "fthd,fthe->fhde", phi_key, value_heads, preferred_element_type=jnp.float32
    )
    total_part = jnp.sum(phi_key, axis=1, dtype=jnp.float32)
    empty = (jnp.zeros((HEADS, HDIM, HDIM), jnp.float32), jnp.zeros((HEADS, HDIM), jnp.float32))
    state_frame, total_frame = (
        lax.psum(state_part.astype(jnp.bfloat16), "rows").astype(jnp.float32),
        lax.psum(total_part.astype(jnp.bfloat16), "rows").astype(jnp.float32),
    )
    carried = prefix(
        (jnp.sum(state_frame, axis=0), jnp.sum(total_frame, axis=0)), "tm", add_pair, empty
    )
    states = carried[0][None] + jnp.cumsum(state_frame, axis=0)
    totals = carried[1][None] + jnp.cumsum(total_frame, axis=0)
    state_low = states.astype(jnp.bfloat16)
    numerator = jnp.einsum(
        "fthd,fhde->fthe", phi_query, state_low, preferred_element_type=jnp.float32
    )
    denominator = jnp.einsum("fthd,fhd->fth", phi_query, totals, preferred_element_type=jnp.float32)
    attended = (numerator / denominator[..., None]).reshape(
        frame_count, row_count, col_count, width
    )
    widened = padded_2(hidden, (("rows", 1),), 1)
    padded = jnp.pad(widened, ((0, 0), (0, 0), (1, 1), (0, 0)))
    accum = jnp.zeros(hidden.shape, jnp.float32) + conv_bias
    for i in range(3):
        for j in range(3):
            accum = (
                accum
                + padded[:, i : i + row_count, j : j + col_count].astype(jnp.float32)
                * conv_weight[i, j]
            )
    half = hidden.shape[3] // 2
    gated = (accum[..., :half] * jax.nn.silu(accum[..., half:])).astype(jnp.bfloat16)
    return (attended, gated)


def solution(mesh):
    in_specs = (
        P("tm", "rows", None, None),
        P("tm", "rows", None, None),
        P("tm", "rows", None, None),
        P("tm", "rows", None, None),
        P(),
        P(),
    )
    out_specs = (P("tm", "rows", None, None), P("tm", "rows", None, None))
    return jax.shard_map(
        on_device, mesh=mesh, in_specs=in_specs, out_specs=out_specs, check_vma=False
    )
```

profile of v0, /device:TPU:1, one launch (start us, length us, event | category | flops | bytes accessed | tf_op | source)
XLA Modules:
  0.0 319.0 jit_solution(14764807090760903211)
XLA Ops:
  7.2 4.6 %reshape.35 = bf16[2,160,20,112]{3,2,1,0:T(8,128)(2,1)} reshape(bf16[2,2,80,2240]{3,2,1,0:T(8,128)(2,1)} %param.10) | data formatting | bytes 2867200 | tf_op jit(solution)/shard_map/reshape | solution.py:59
  11.8 2.8 fusion.31
  14.7 3.1 reshape.34
  17.7 4.0 %fusion.20 = bf16[2,20,112,112]{3,2,1,0:T(8,128)(2,1)} fusion(bf16[2,160,20,112]{3,2,1,0:T(8,128)(2,1)} %reshape.35, bf16[2,160,20,112]{3,2,1,0:T(8,128)(2,1)} %reshape.34), kind=kOutput, calls=%fused_computation.32 | convolution fusion | flops 161064960 | bytes 3870720 | tf_op jit(solution)/shard_map/fthd,fthe->fhde/dot_general | solution.py:60
  21.9 69.7 %all-reduce.3.cloned.1.call-done = bf16[2,20,112,112]{3,2,1,0:T(8,128)(2,1)} async-done(((bf16[2,20,112,112]{3,2,1,0:T(8,128)(2,1)}), bf16[2,20,112,112]{3,2,1,0:T(8,128)(2,1)}) %all-reduce.3.cloned.1.call-update) | async-done | bytes 1003536 | tf_op jit(solution)/shard_map/psum | solution.py:66
  91.6 2.5 reduce_sum.38
  94.1 4.1 %fusion.33 = (bf16[2,1,80,5600]{3,2,1,0:T(8,128)(2,1)}, bf16[2,1,80,5600]{3,2,1,0:T(8,128)(2,1)}) fusion(bf16[2,2,80,5600]{3,2,1,0:T(8,128)(2,1)} %param.11), kind=kLoop, calls=%fused_computation.51 | loop fusion | bytes 7168000 | tf_op jit(solution)/shard_map/slice | solution.py:39
  98.2 4.8 %collective-permute-start.1 = (bf16[2,1,80,5600]{3,2,1,0:T(8,128)(2,1)}, bf16[2,1,80,5600]{3,2,1,0:T(8,128)(2,1)S(1)}, u32[]{:S(2)}, u32[]{:S(2)}) collective-permute-start(bf16[2,1,80,5600]{3,2,1,0:T(8,128)(2,1)} %get-tuple-element.159), channel_id=1, source_target_pairs={{1,0},{2,1},{3,2},{4,3},{5,4},{6,5},{7,6},{9,8},{10,9},{11,10},{12... | collective-permute-start | bytes 5376008 | tf_op jit(solution)/shard_map/ppermute | solution.py:41
  103.0 1.9 collective-permute-start
  105.1 35.8 %psum.15 = bf16[2,20,112]{2,1,0:T(8,128)(2,1)S(1)} all-reduce(bf16[2,20,112]{2,1,0:T(8,128)(2,1)S(1)} %reduce_sum.40), channel_id=1, replica_groups=mesh['tm'=32,'rows'=8] {'rows'}, use_global_device_ids=true, to_apply=%region_3.4 | all-reduce | flops 4480 | bytes 17920 | tf_op jit(solution)/shard_map/psum | solution.py:67
  140.9 3.8 %fusion.12 = bf16[2,2,80,2240]{3,2,1,0:T(8,128)(2,1)} fusion(bf16[2,2,80,2240]{3,2,1,0:T(8,128)(2,1)} %param.8), kind=kLoop, calls=%fused_computation.25 | loop fusion | flops 4300800 | bytes 2867200 | tf_op jit(solution)/shard_map/convert_element_type | solution.py:47
  144.8 4.6 %reshape.36 = bf16[2,160,20,112]{3,2,1,0:T(8,128)(2,1)} reshape(bf16[2,2,80,2240]{3,2,1,0:T(8,128)(2,1)} %fusion.12) | data formatting | bytes 2867200 | tf_op jit(solution)/shard_map/reshape | solution.py:57
  149.3 42.7 %all-gather.2 = bf16[32,20,112]{2,1,0:T(8,128)(2,1)S(1)} all-gather(bf16[1,20,112]{2,1,0:T(8,128)(2,1)S(1)} %bitcast.30), channel_id=3, replica_groups=mesh['tm'=32,'rows'=8] {'tm'}, dimensions={0}, use_global_device_ids=true | all-gather | bytes 147840 | tf_op jit(solution)/shard_map/all_gather | solution.py:13
  192.1 1.9 slice_reduce_fusion.8
  194.0 5.2 %fusion.5 = bf16[2,4,82,5600]{3,2,1,0:T(8,128)(2,1)S(1)} fusion(bf16[2,1,80,5600]{3,2,1,0:T(8,128)(2,1)S(1)} %collective-permute-done.1, bf16[2,2,80,5600]{3,2,1,0:T(8,128)(2,1)} %param.11, bf16[2,1,80,5600]{3,2,1,0:T(8,128)(2,1)} %collective-permute-done), kind=kLoop, calls=%fused_computation.13 | loop fusion | flops 44083200 | bytes 14515200 | tf_op jit(solution)/shard_map/concatenate | solution.py:42
  199.2 8.7 %multiply_add_fusion = f32[2,2,80,5600]{3,2,1,0:T(8,128)S(1)} fusion(bf16[2,2,80,5600]{3,2,1,0:T(8,128)(2,1)S(1)} %copy-done, bf16[2,4,82,5600]{3,2,1,0:T(8,128)(2,1)S(1)} %fusion.5, bf16[2,1,80,5600]{3,2,1,0:T(8,128)(2,1)S(1)} %collective-permute-done.1, bf16[2,1,80,5600]{3,2,1,0:T(8,128)(2,1)} %collective-permute-done, f32[5600]{0:T(1024)S(1)} %get-tuple-element.142, ...), kind=kLoop, calls=%fused_computation.14 | loop fusion | flops 51968000 | bytes 36064000 | tf_op jit(solution)/shard_map/add | solution.py:88
  207.9 2.5 fusion.6
  210.4 34.2 %all-gather.5.cloned.1.call-done = bf16[640,112,112]{2,1,0:T(8,128)(2,1)} async-done(((bf16[20,112,112]{2,1,0:T(8,128)(2,1)}), bf16[640,112,112]{2,1,0:T(8,128)(2,1)}) %all-gather.5.cloned.1.call-update) | async-done | bytes 16056336 | tf_op jit(solution)/shard_map/all_gather | solution.py:13
  244.7 54.6 %while.16 = (s32[]{:T(128)}, f32[20,112,112]{2,1,0:T(8,128)S(1)}, f32[20,112]{1,0:T(8,128)S(1)}, s32[]{:T(128)}, bf16[32,20,112,112]{3,2,1,0:T(8,128)(2,1)}, /*i...) while((s32[]{:T(128)}, f32[20,112,112]{2,1,0:T(8,128)S(1)}, f32[20,112]{1,0:T(8,128)S(1)}, ...), condition=%wide.region_6.7_spmd.clone, body=%wide.region_5.6_spmd.clone.sunk | while | flops 1012484 | bytes 2531323 | solution.py:30
  244.7 1.8 add_select_fusion.4
  246.5 1.7 add_select_fusion.4
  248.2 1.7 add_select_fusion.4
  249.9 1.7 add_select_fusion.4
  251.6 1.7 add_select_fusion.4
  253.3 1.7 add_select_fusion.4
  255.0 1.7 add_select_fusion.4
  256.7 1.7 add_select_fusion.4
  258.4 1.7 add_select_fusion.4
  260.1 1.7 add_select_fusion.4
  261.8 1.7 add_select_fusion.4
  263.5 1.7 add_select_fusion.4
  265.2 1.7 add_select_fusion.4
  266.9 1.7 add_select_fusion.4
  268.6 1.7 add_select_fusion.4
  270.3 1.7 add_select_fusion.4
  272.0 1.7 add_select_fusion.4
  273.8 1.7 add_select_fusion.4
  275.5 1.7 add_select_fusion.4
  277.2 1.7 add_select_fusion.4
  278.9 1.7 add_select_fusion.4
  280.6 1.7 add_select_fusion.4
  282.3 1.7 add_select_fusion.4
  284.0 1.7 add_select_fusion.4
  285.7 1.7 add_select_fusion.4
  287.4 1.7 add_select_fusion.4
  289.1 1.7 add_select_fusion.4
  303.4 3.8 %copy.18 = f32[2,160,20,112]{3,2,1,0:T(8,128)} copy(f32[2,160,20,112]{3,1,2,0:T(8,128)S(1)} %bitcast_divide_fusion) | data formatting | bytes 5734400 | tf_op jit(solution)/shard_map/div | solution.py:79
  307.2 5.0 %reshape.37 = f32[2,2,80,2240]{3,2,1,0:T(8,128)} reshape(f32[2,160,20,112]{3,2,1,0:T(8,128)} %copy.18) | data formatting | bytes 5734400 | tf_op jit(solution)/shard_map/reshape | solution.py:79
  (58 shorter events, 13.1 us)
Async XLA Ops:
  7.2 84.4 %all-reduce.3.cloned.1.call-start = ((), (), s32[]{:S(2)}) async-start(), calls=%async_computation | async-start | bytes 2293760 | tf_op jit(solution)/shard_map/psum | solution.py:66
  21.8 222.8 %all-gather.5.cloned.1.call-start = ((), (), s32[]{:S(2)}) async-start(), calls=%async_computation.1 | async-start | bytes 18923520 | tf_op jit(solution)/shard_map/all_gather | solution.py:13
  98.2 95.8 %collective-permute-start.1 = (bf16[2,1,80,5600]{3,2,1,0:T(8,128)(2,1)}, bf16[2,1,80,5600]{3,2,1,0:T(8,128)(2,1)S(1)}, u32[]{:S(2)}, u32[]{:S(2)}) collective-permute-start(bf16[2,1,80,5600]{3,2,1,0:T(8,128)(2,1)} %get-tuple-element.159), channel_id=1, source_target_pairs={{1,0},{2,1},{3,2},{4,3},{5,4},{6,5},{7,6},{9,8},{10,9},{11,10},{12... | collective-permute-start | bytes 5376008 | tf_op jit(solution)/shard_map/ppermute | solution.py:41
  103.0 91.0 %collective-permute-start = (bf16[2,1,80,5600]{3,2,1,0:T(8,128)(2,1)}, bf16[2,1,80,5600]{3,2,1,0:T(8,128)(2,1)}, u32[]{:S(2)}, u32[]{:S(2)}) collective-permute-start(bf16[2,1,80,5600]{3,2,1,0:T(8,128)(2,1)} %get-tuple-element.158), channel_id=1, source_target_pairs={{0,1},{1,2},{2,3},{3,4},{4,5},{5,6},{6,7},{8,9},{9,10},{10,11},{11... | collective-permute-start | bytes 5376008 | tf_op jit(solution)/shard_map/ppermute | solution.py:38
  194.0 5.2 %copy-start = (bf16[2,2,80,5600]{3,2,1,0:T(8,128)(2,1)S(1)}, bf16[2,2,80,5600]{3,2,1,0:T(8,128)(2,1)}, u32[]{:S(2)}) copy-start(bf16[2,2,80,5600]{3,2,1,0:T(8,128)(2,1)} %param.11) | copy-start | bytes 10752004
  194.0 5.2 %copy-start.2 = (f32[5600]{0:T(1024)S(1)}, f32[5600]{0:T(1024)}, u32[]{:S(2)}) copy-start(f32[5600]{0:T(1024)} %param.13) | copy-start | bytes 67204
  244.6 54.7 %copy-start.1 = (bf16[2,160,20,112]{3,2,1,0:T(8,128)(2,1)S(1)}, bf16[2,160,20,112]{3,2,1,0:T(8,128)(2,1)}, u32[]{:S(2)}) copy-start(bf16[2,160,20,112]{3,2,1,0:T(8,128)(2,1)} %reshape.36) | copy-start | bytes 4300804
Sparse Core Ops, SparseCore 0:
  21.9 69.6 all-reduce.2
  94.2 150.3 all-gather.4
where the time goes:
time: 321 us; the launch traced here: 319 us
  waiting for transfers between devices  104 us (32%)
  other arithmetic  80.8 us (25%)
  blocking collectives  78.6 us (24%)
  local copies, waits for them, and re-layouts  27.1 us (8%)
  between operations  14.2 us (4%)
  starting transfers between devices  6.83 us (2%)
  matrix products  6.5 us (2%)
    psum x1, waiting for transfers between devices, on_device(): lax.psum(state_part.astype(jnp.bfloat16), 'rows').astype(jnp.float32)  69.7 us
    select_n x64, other arithmetic, lap(): return jax.tree.map(lambda a, b: jnp.where(reached, a, b), new, before)  53.7 us
    all_gather x1, blocking collectives, prefix(): lax.all_gather(part.astype(kind), axis)  42.7 us
    psum x1, blocking collectives, on_device(): lax.psum(total_part.astype(jnp.bfloat16), 'rows').astype(jnp.float32)  35.8 us
    all_gather x1, waiting for transfers between devices, prefix(): lax.all_gather(part.astype(kind), axis)  34.2 us
    add x1, other arithmetic, on_device(): accum + padded[:, i:i + row_count, j:j + col_count].astype(jnp.float32) *...  8.74 us
  transfers between devices with their start and end apart: 4, of which 2 were waited for; matrix products, arithmetic and copies ran while one was open for 10% of the time, Pallas kernels for 0%

commit v1 on v0

v1 whole, which is shorter than its diff:
```python
import jax
import jax.numpy as jnp
from jax import lax
from jax.experimental import pallas as pl
from jax.experimental.pallas import tpu as pltpu
from jax.sharding import PartitionSpec as P

HEADS = 20
HDIM = 112
WIDTH = HEADS * HDIM
HALF = 2800
FULL = 2 * HALF
COLS = 80
TOK = 2 * COLS
LT = 18
LPAD = LT * 128
HT = LT // 2
BLK = 1024
TOTROW = HT * HDIM
QTR = BLK // 4
SL = QTR // 8
MESH = pl.DeviceIdType.MESH
CUTS = (0, 4, 8, 12, 16, 19, 22)
NP = len(CUTS) - 1


def val_lanes(k):
    lo, hi = CUTS[k], min(CUTS[k + 1], 21)
    return lo * 128, (hi - lo) * 128


def gate_lanes(k):
    lo = 21 if k == 0 else 22 + CUTS[k]
    hi = min(22 + CUTS[k + 1], 44)
    start, end = lo * 128, min(hi * 128, FULL)
    return start, end - start


def features(x):
    x = x.astype(jnp.float32)
    return jnp.where(x > 0, x + 1.0, jnp.exp(x)).astype(jnp.bfloat16)


def kernel(
    q_hbm, k_hbm, v_hbm, h_hbm, w_hbm, b_hbm,
    att_hbm, gat_hbm,
    q_v, k_v, v_v, h_v, w_v, b_v, up_v, dn_v,
    dense, state, send_c, recv_c, send_a, recv_a, send_b, recv_b, own,
    send_z, recv_z, send_x, recv_x, send_e, recv_e, final, wide, att_v, gat_v,
    load_sem, kv_sem, out_sem, halo_s, halo_r, c_s, c_r, a_s, a_r, b_s, b_r,
    z_s, z_r, x_s, x_r, e_s, e_r, g_s, g_r, f_s, f_r,
):
    tm = lax.axis_index("tm")
    row = lax.axis_index("rows")
    x, z = tm // 8, tm % 8
    y, c = row // 2, row % 2
    sib = (tm, row + 1 - 2 * c)
    alpha = y + 1 - 2 * (y % 2)
    beta = 3 - y
    opp = (y + 2) % 4
    dev_a, dev_b = (tm, alpha * 2 + c), (tm, beta * 2 + c)
    above, below = (tm, (row + 7) % 8), (tm, (row + 1) % 8)
    zdev = [(x * 8 + (z + d) % 8, row) for d in range(8)]
    xdev = [(((x + d) % 4) * 8 + z, row) for d in range(4)]

    def load(src, dst, sem):
        copy = pltpu.make_async_copy(src, dst, sem)
        copy.start()
        return copy

    kv = [
        (load(k_hbm.at[f], k_v.at[f], kv_sem.at[f, 0]), load(v_hbm.at[f], v_v.at[f], kv_sem.at[f, 1]))
        for f in range(2)
    ]
    load_h = load(h_hbm, h_v, load_sem.at[0])
    load_q = load(q_hbm, q_v, load_sem.at[1])
    load_w = load(w_hbm, w_v, load_sem.at[2])
    load_b = load(b_hbm, b_v, load_sem.at[3])

    barrier = pltpu.get_barrier_semaphore()
    partners = [above, below, dev_a, dev_b] + zdev[1:] + xdev[1:]
    for device in partners:
        pl.semaphore_signal(barrier, inc=1, device_id=device, device_id_type=MESH)
    pl.semaphore_wait(barrier, len(partners))

    def remote(src, dst, ss, rs, device):
        return pltpu.make_async_remote_copy(
            src_ref=src, dst_ref=dst, send_sem=ss, recv_sem=rs, device_id=device, device_id_type=MESH
        )

    def halo(k):
        copies = []
        for n, (start, size) in enumerate((val_lanes(k), gate_lanes(k))):
            lanes = pl.ds(start, size)
            copies.append(remote(h_hbm.at[:, 1, :, lanes], up_v.at[:, :, lanes],
                                 halo_s.at[k, n, 0], halo_r.at[k, n, 0], below))
            copies.append(remote(h_hbm.at[:, 0, :, lanes], dn_v.at[:, :, lanes],
                                 halo_s.at[k, n, 1], halo_r.at[k, n, 1], above))
        return copies

    halos = [halo(k) for k in range(NP)]

    def start(copies):
        for copy in copies:
            copy.start()

    for k in range(NP):
        start(halos[k])

    lane = lax.broadcasted_iota(jnp.int32, (HDIM, 2 * HDIM), 1)
    sends = []
    core = []
    for f in range(2):
        kv[f][0].wait()
        kv[f][1].wait()
        phi = features(k_v[f].reshape(TOK, WIDTH))
        val = v_v[f].reshape(TOK, WIDTH)
        dense[:, LPAD - 128:] = jnp.zeros((HDIM, 128), jnp.float32)
        for p in range(HEADS // 2):
            lo = 2 * HDIM * p
            prod = lax.dot_general(
                phi[:, lo:lo + 2 * HDIM], val[:, lo:lo + 2 * HDIM], (((0,), (0,)), ((), ())),
                preferred_element_type=jnp.float32,
            )
            dense[:, lo:lo + 2 * HDIM] = jnp.where(lane < HDIM, prod[:HDIM], prod[HDIM:])
        total = jnp.sum(phi.astype(jnp.float32), axis=0, keepdims=True)
        total = jnp.concatenate([total, jnp.zeros((1, LPAD - WIDTH), jnp.float32)], axis=1)
        for l in range(LT):
            half, at = l // HT, l % HT
            state[f, half, at * HDIM:(at + 1) * HDIM] = dense[:, l * 128:(l + 1) * 128]
        for half in range(2):
            rows = [total[:, l * 128:(l + 1) * 128] for l in range(half * HT, (half + 1) * HT)]
            rows.append(jnp.zeros((BLK - TOTROW - HT, 128), jnp.float32))
            state[f, half, TOTROW:] = jnp.concatenate(rows, axis=0)
        send_c[f] = state[f, 1 - c].astype(jnp.bfloat16)
        copy = remote(send_c.at[f], recv_c.at[f], c_s.at[f], c_r.at[f], sib)
        copy.start()
        core.append(copy)

    load_h.wait()
    load_w.wait()
    load_b.wait()
    top = jnp.where(row > 0, 1.0, 0.0)
    bottom = jnp.where(row < 7, 1.0, 0.0)
    shift = FULL - HALF - 22 * 128 + 128
    col8 = lax.broadcasted_iota(jnp.int32, (8, 128), 0)

    def conv_tile(f, src, n, take):
        rows = [up_v[f, :, src], h_v[f, 0, :, src], h_v[f, 1, :, src], dn_v[f, :, src]]
        rows = [take(r).astype(jnp.float32) for r in rows]
        bias = take(b_v[:, src])
        weight = [take(w_v[i, :, src]) for i in range(3)]
        first, last = [weight[0] * top, weight[1], weight[2]], [weight[0], weight[1], weight[2] * bottom]
        outs = []
        for o, weights in ((0, first), (1, last)):
            parts = []
            for j in range(3):
                parts.append(sum(rows[o + i] * weights[i][j:j + 1] for i in range(3)))
            edge = col8[:, :n]
            left = jnp.concatenate([parts[0][:72], jnp.where(edge < 7, parts[0][72:], 0.0)], axis=0)
            right = jnp.concatenate([jnp.where(edge > 0, parts[2][:8], 0.0), parts[2][8:]], axis=0)
            outs.append(parts[1] + bias + pltpu.roll(left, 1, 0) + pltpu.roll(right, COLS - 1, 0))
        return outs

    def conv_out(f, a, n):
        gate_at = (21 + a) * 128
        if n == 128:
            gate_src = pl.ds(pl.multiple_of(gate_at, 128), 256)
            value_src = pl.ds(pl.multiple_of(a * 128, 128), 128)
        else:
            gate_src = pl.ds(gate_at, FULL - gate_at)
            value_src = pl.ds(a * 128, 128)
        gate = conv_tile(f, gate_src, n, lambda r: r[:, shift:shift + n])
        value = conv_tile(f, value_src, n, lambda r: r[:, :n])
        for o in range(2):
            gated = value[o] * (gate[o] / (1.0 + jnp.exp(-gate[o])))
            gat_v[f, o, :, pl.ds(a * 128 if n < 128 else pl.multiple_of(a * 128, 128), n)] = gated.astype(jnp.bfloat16)

    def conv(k):
        for copy in halos[k]:
            copy.wait_recv()
        lo, hi = CUTS[k], min(CUTS[k + 1], 21)

        @pl.loop(0, 2)
        def _(f):
            @pl.loop(lo, hi)
            def _(a):
                conv_out(f, a, 128)

            if CUTS[k + 1] == 22:
                conv_out(f, 21, HALF - 21 * 128)

    hops = ((alpha, dev_a, beta, dev_b), (beta, dev_b, alpha, dev_a))

    def quarter(q):
        return pl.ds(pl.multiple_of(q * QTR, QTR), QTR)

    step_a = []
    for f in range(2):
        first, dev, second, _ = hops[f]
        core[f].wait_recv()
        for n, q in ((0, first), (1, opp)):
            send_a[f, n] = (state[f, c, quarter(q)] + recv_c[f, quarter(q)].astype(jnp.float32)).astype(jnp.bfloat16)
        copy = remote(send_a.at[f], recv_a.at[f], a_s.at[f], a_r.at[f], dev)
        copy.start()
        step_a.append(copy)
    conv(0)
    step_b = []
    for f in range(2):
        first, _, second, dev = hops[f]
        step_a[f].wait_recv()
        q = quarter(second)
        send_b[f] = (state[f, c, q] + recv_c[f, q].astype(jnp.float32) + recv_a[f, 1].astype(jnp.float32)).astype(jnp.bfloat16)
        copy = remote(send_b.at[f], recv_b.at[f], b_s.at[f], b_r.at[f], dev)
        copy.start()
        step_b.append(copy)
        q = quarter(y)
        own[f] = state[f, c, q] + recv_c[f, q].astype(jnp.float32) + recv_a[f, 0].astype(jnp.float32)
    conv(1)
    for f in range(2):
        step_b[f].wait_recv()
        own[f] = own[f] + recv_b[f].astype(jnp.float32)

    send_z[...] = (own[0] + own[1]).astype(jnp.bfloat16).reshape(8, SL, 128)
    step_z = []
    for d in (4, 3, 5, 2, 6, 1, 7):
        copy = remote(send_z.at[(z + d) % 8], recv_z.at[z], z_s.at[d - 1], z_r.at[d - 1], zdev[d])
        copy.start()
        step_z.append(copy)
    recv_z[z] = send_z[z]
    conv(2)
    for copy in step_z:
        copy.wait_recv()
    send_x[...] = sum(recv_z[j].astype(jnp.float32) for j in range(8)).astype(jnp.bfloat16)
    step_x = []
    for d in (2, 1, 3):
        copy = remote(send_x, recv_x.at[x], x_s.at[d - 1], x_r.at[d - 1], xdev[d])
        copy.start()
        step_x.append(copy)
    recv_x[x] = jnp.zeros((SL, 128), jnp.bfloat16)
    conv(3)
    for copy in step_x:
        copy.wait_recv()
    running = jnp.zeros((SL, 128), jnp.float32)
    for i in range(4):
        running = running + jnp.where(i < x, recv_x[i].astype(jnp.float32), 0.0)
    for j in range(8):
        send_e[j] = running.astype(jnp.bfloat16)
        running = running + recv_z[j].astype(jnp.float32)
    step_e = []
    for d in (4, 3, 5, 2, 6, 1, 7):
        copy = remote(send_e.at[(z + d) % 8], recv_e.at[z], e_s.at[d - 1], e_r.at[d - 1], zdev[d])
        copy.start()
        step_e.append(copy)
    recv_e[z] = send_e[z]
    load_q.wait()
    conv(4)
    for copy in step_e:
        copy.wait_recv()

    before = recv_e[...].reshape(QTR, 128).astype(jnp.float32)
    states = before + own[0]
    final[0, c, quarter(y)] = states.astype(jnp.bfloat16)
    final[1, c, quarter(y)] = (states + own[1]).astype(jnp.bfloat16)

    forwards = [[], []]

    def spread(f, q, dev, ss, rs):
        ref = final.at[f, c, quarter(q)]
        copy = remote(ref, ref, ss, rs, dev)
        copy.start()
        return copy

    def forward(f, q):
        n = len(forwards[f])
        forwards[f].append(spread(f, q, sib, f_s.at[f, n], f_r.at[f, n]))

    step_g = [[], []]
    for f in range(2):
        first, dev1, second, dev2 = hops[f]
        step_g[f].append(spread(f, y, dev2, g_s.at[f, 0], g_r.at[f, 0]))
        step_g[f].append(spread(f, y, dev1, g_s.at[f, 1], g_r.at[f, 1]))
    for f in range(2):
        forward(f, y)
    for f in range(2):
        first, dev1, second, dev2 = hops[f]
        step_g[f][0].wait_recv()
        step_g[f].append(spread(f, second, dev1, g_s.at[f, 2], g_r.at[f, 2]))
        forward(f, second)
    conv(5)
    for f in range(2):
        first, dev1, second, dev2 = hops[f]
        step_g[f][1].wait_recv()
        forward(f, first)
    for f in range(2):
        step_g[f][2].wait_recv()
        forward(f, opp)
    out_g = load(gat_v, gat_hbm, out_sem.at[0])

    same = (lax.broadcasted_iota(jnp.int32, (2 * HDIM, 2 * HDIM), 0) < HDIM) == (
        lax.broadcasted_iota(jnp.int32, (2 * HDIM, 2 * HDIM), 1) < HDIM
    )
    ones = jnp.where(same, 1.0, 0.0).astype(jnp.bfloat16)
    out_a = []
    for f in range(2):
        for copy in forwards[f]:
            copy.wait_recv()
        for l in range(LT):
            half, at = l // HT, l % HT
            wide[:, l * 128:(l + 1) * 128] = final[f, half, at * HDIM:(at + 1) * HDIM]
        tails = [final[f, half, TOTROW:].astype(jnp.float32) for half in range(2)]
        total = jnp.concatenate([tails[l // HT][l % HT:l % HT + 1] for l in range(LT)], axis=1)[:, :WIDTH]
        phi = features(q_v[f].reshape(TOK, WIDTH))
        scaled = (phi.astype(jnp.float32) * total).astype(jnp.bfloat16)
        for p in range(HEADS // 2):
            lo = 2 * HDIM * p
            block = wide[:, lo:lo + 2 * HDIM]
            block = jnp.concatenate([block, block], axis=0)
            block = jnp.where(same, block, jnp.zeros_like(block))
            num = jnp.dot(phi[:, lo:lo + 2 * HDIM], block, preferred_element_type=jnp.float32)
            den = jnp.dot(scaled[:, lo:lo + 2 * HDIM], ones, preferred_element_type=jnp.float32)
            att_v[f, :, :, lo:lo + 2 * HDIM] = (num / den).reshape(2, COLS, 2 * HDIM)
        out_a.append(load(att_v.at[f], att_hbm.at[f], out_sem.at[1 + f]))

    for copies in halos + [core, step_a, step_b, step_z, step_x, step_e] + step_g + forwards:
        for copy in copies:
            copy.wait_send()
    out_g.wait()
    for copy in out_a:
        copy.wait()


def on_device(queries, key_rows, value_rows, hidden, conv_weight, conv_bias):
    bf, f32 = jnp.bfloat16, jnp.float32
    vmem, dma = pltpu.VMEM, pltpu.SemaphoreType.DMA
    hbm = pl.BlockSpec(memory_space=pl.ANY)
    return pl.pallas_call(
        kernel,
        out_shape=(
            jax.ShapeDtypeStruct((2, 2, COLS, WIDTH), f32),
            jax.ShapeDtypeStruct((2, 2, COLS, HALF), bf),
        ),
        in_specs=[hbm] * 6,
        out_specs=(hbm, hbm),
        scratch_shapes=[
            vmem((2, 2, COLS, WIDTH), bf), vmem((2, 2, COLS, WIDTH), bf), vmem((2, 2, COLS, WIDTH), bf),
            vmem((2, 2, COLS, FULL), bf), vmem((3, 3, FULL), f32), vmem((1, FULL), f32),
            vmem((2, COLS, FULL), bf), vmem((2, COLS, FULL), bf),
            vmem((HDIM, LPAD), f32), vmem((2, 2, BLK, 128), f32),
            vmem((2, BLK, 128), bf), vmem((2, BLK, 128), bf),
            vmem((2, 2, QTR, 128), bf), vmem((2, 2, QTR, 128), bf),
            vmem((2, QTR, 128), bf), vmem((2, QTR, 128), bf), vmem((2, QTR, 128), f32),
            vmem((8, SL, 128), bf), vmem((8, SL, 128), bf),
            vmem((SL, 128), bf), vmem((4, SL, 128), bf),
            vmem((8, SL, 128), bf), vmem((8, SL, 128), bf),
            vmem((2, 2, BLK, 128), bf), vmem((HDIM, LPAD), bf),
            vmem((2, 2, COLS, WIDTH), f32), vmem((2, 2, COLS, HALF), bf),
            dma((4,)), dma((2, 2)), dma((3,)), dma((NP, 2, 2)), dma((NP, 2, 2)),
            dma((2,)), dma((2,)), dma((2,)), dma((2,)), dma((2,)), dma((2,)),
            dma((7,)), dma((7,)), dma((3,)), dma((3,)), dma((7,)), dma((7,)),
            dma((2, 3)), dma((2, 3)), dma((2, 4)), dma((2, 4)),
        ],
        compiler_params=pltpu.CompilerParams(
            collective_id=0, has_side_effects=True, vmem_limit_bytes=48 * 1024 * 1024
        ),
        name="linear_attention_conv",
    )(queries, key_rows, value_rows, hidden, conv_weight, conv_bias.reshape(1, FULL))


def solution(mesh):
    block = P("tm", "rows", None, None)
    return jax.shard_map(
        on_device, mesh=mesh, in_specs=(block, block, block, block, P(), P()),
        out_specs=(block, block), check_vma=False,
    )
```

time: 321 us -> 78.7 us (0.25)
  waiting for transfers between devices: 104 us -> 0 us
  other arithmetic: 80.8 us -> 0 us
  blocking collectives: 78.6 us -> 0 us
  Pallas kernels: 0 us -> 66.8 us
  local copies, waits for them, and re-layouts: 27.1 us -> 10.9 us
  between operations: 14.2 us -> 0.66 us
  starting transfers between devices: 6.83 us -> 0 us
  matrix products: 6.5 us -> 0 us
    psum x1 -> x0, waiting for transfers between devices: 69.7 us -> none  [on_device(): lax.psum(state_part.astype(jnp.bfloat16), 'rows').astype(jnp.float32)]
    pallas_call x0 -> x1, Pallas kernels: none -> 66.8 us  [on_device(): pl.pallas_call(kernel, out_shape=(jax.ShapeDtypeStruct((2, 2, COLS, WIDTH...]
    select_n x64 -> x0, other arithmetic: 53.7 us -> none  [lap(): return jax.tree.map(lambda a, b: jnp.where(reached, a, b), new, before)]
    all_gather x1 -> x0, blocking collectives: 42.7 us -> none  [prefix(): lax.all_gather(part.astype(kind), axis)]
    psum x1 -> x0, blocking collectives: 35.8 us -> none  [on_device(): lax.psum(total_part.astype(jnp.bfloat16), 'rows').astype(jnp.float32)]
    all_gather x1 -> x0, waiting for transfers between devices: 34.2 us -> none  [prefix(): lax.all_gather(part.astype(kind), axis)]
    reshape x4 -> x1, local copies, waits for them, and re-layouts: 17.3 us -> 0.75 us  [on_device(): conv_bias.reshape(1, FULL)]
    unnamed x6 -> x12, local copies, waits for them, and re-layouts: 0.02 us -> 10.1 us
  transfers between devices with their start and end apart: 4 -> 0, of which waited for: 2 -> 0; matrix products, arithmetic and copies ran while one was open for 10% -> 0% of each run, Pallas kernels for 0% -> 0%
where the time goes in v1:
time: 78.7 us; the launch traced here: 78.4 us
  Pallas kernels  66.8 us (85%)
  local copies, waits for them, and re-layouts  10.9 us (14%)
    pallas_call x1, Pallas kernels, on_device(): pl.pallas_call(kernel, out_shape=(jax.ShapeDtypeStruct((2, 2, COLS, WIDTH...  66.8 us
    unnamed x12, local copies, waits for them, and re-layouts  10.1 us

profile of v1, /device:TPU:1, one launch (start us, length us, event | category | flops | bytes accessed | tf_op | source)
XLA Modules:
  0.0 78.4 jit_solution(5175332946654706195)
XLA Ops:
  0.6 0.8 reshape.7.b_hbm
  1.4 0.0 copy-start
  1.4 1.4 %copy-done = bf16[2,2,80,2240]{3,2,1,0:T(8,128)(2,1)S(1)} copy-done((bf16[2,2,80,2240]{3,2,1,0:T(8,128)(2,1)S(1)}, bf16[2,2,80,2240]{3,2,1,0:T(8,128)(2,1)}, u32[]{:S(2)}) %copy-start) | copy-done | bytes 1433624
  2.8 0.0 copy-start.1
  2.8 1.4 %copy-done.1 = bf16[2,2,80,2240]{3,2,1,0:T(8,128)(2,1)S(1)} copy-done((bf16[2,2,80,2240]{3,2,1,0:T(8,128)(2,1)S(1)}, bf16[2,2,80,2240]{3,2,1,0:T(8,128)(2,1)}, u32[]{:S(2)}) %copy-start.1) | copy-done | bytes 1433624
  4.1 0.0 copy-start.2
  4.1 1.4 %copy-done.2 = bf16[2,2,80,2240]{3,2,1,0:T(8,128)(2,1)S(1)} copy-done((bf16[2,2,80,2240]{3,2,1,0:T(8,128)(2,1)S(1)}, bf16[2,2,80,2240]{3,2,1,0:T(8,128)(2,1)}, u32[]{:S(2)}) %copy-start.2) | copy-done | bytes 1433624
  5.5 0.0 copy-start.3
  5.5 1.0 %copy-done.3 = f32[3,3,5600]{2,1,0:T(4,128)S(1)} copy-done((f32[3,3,5600]{2,1,0:T(4,128)S(1)}, f32[3,3,5600]{2,1,0:T(4,128)}, u32[]{:S(2)}) %copy-start.3) | copy-done | bytes 201624
  6.5 66.8 %linear_attention_conv.1 = (f32[2,2,80,2240]{3,2,1,0:T(8,128)}, bf16[2,2,80,2800]{3,2,1,0:T(8,128)(2,1)}) custom-call(bf16[2,2,80,2240]{3,2,1,0:T(8,128)(2,1)S(1)} %copy-done, bf16[2,2,80,2240]{3,2,1,0:T(8,128)(2,1)S(1)} %copy-done.1, bf16[2,2,80,2240]{3,2,1,0:T(8,128)(2,1)S(1)} %copy-done.2, bf16[2,2,80,5600]{3,2,1,0:T(8,128)(2,1)} %h_hbm.1, ...), custom_call_target="tpu_custom_call" | custom-call | tf_op jit(solution)/shard_map/linear_attention_conv/pallas_call | solution.py:337
  73.3 0.0 copy-start.4
  73.3 3.8 %copy.10 = f32[2,2,80,2240]{3,2,1,0:T(8,128)} copy(f32[2,2,80,2240]{3,2,1,0:T(8,128)} %get-tuple-element.4) | data formatting | bytes 5734400
  77.2 0.0 copy-done.4
  77.2 1.2 %copy.11 = bf16[2,2,80,2800]{3,2,1,0:T(8,128)(2,1)} copy(bf16[2,2,80,2800]{3,2,1,0:T(8,128)(2,1)S(1)} %copy-done.4) | data formatting | bytes 3584000
Async XLA Ops:
  1.4 1.4 %copy-start = (bf16[2,2,80,2240]{3,2,1,0:T(8,128)(2,1)S(1)}, bf16[2,2,80,2240]{3,2,1,0:T(8,128)(2,1)}, u32[]{:S(2)}) copy-start(bf16[2,2,80,2240]{3,2,1,0:T(8,128)(2,1)} %q_hbm.1) | copy-start | bytes 4300804
  2.8 1.4 %copy-start.1 = (bf16[2,2,80,2240]{3,2,1,0:T(8,128)(2,1)S(1)}, bf16[2,2,80,2240]{3,2,1,0:T(8,128)(2,1)}, u32[]{:S(2)}) copy-start(bf16[2,2,80,2240]{3,2,1,0:T(8,128)(2,1)} %k_hbm.1) | copy-start | bytes 4300804
  4.1 1.4 %copy-start.2 = (bf16[2,2,80,2240]{3,2,1,0:T(8,128)(2,1)S(1)}, bf16[2,2,80,2240]{3,2,1,0:T(8,128)(2,1)}, u32[]{:S(2)}) copy-start(bf16[2,2,80,2240]{3,2,1,0:T(8,128)(2,1)} %v_hbm.1) | copy-start | bytes 4300804
  5.5 1.0 %copy-start.3 = (f32[3,3,5600]{2,1,0:T(4,128)S(1)}, f32[3,3,5600]{2,1,0:T(4,128)}, u32[]{:S(2)}) copy-start(f32[3,3,5600]{2,1,0:T(4,128)} %w_hbm.1) | copy-start | bytes 604804
  73.3 3.9 %copy-start.4 = (bf16[2,2,80,2800]{3,2,1,0:T(8,128)(2,1)S(1)}, bf16[2,2,80,2800]{3,2,1,0:T(8,128)(2,1)}, u32[]{:S(2)}) copy-start(bf16[2,2,80,2800]{3,2,1,0:T(8,128)(2,1)} %get-tuple-element.5) | copy-start | bytes 5376004

commit v2 on v1

--- a/solution.py
+++ b/solution.py
@@ -22,6 +22,7 @@
 MESH = pl.DeviceIdType.MESH
 CUTS = (0, 4, 8, 12, 16, 19, 22)
 NP = len(CUTS) - 1
+VMEM_BYTES = 56 * 1024 * 1024
 
 
 def val_lanes(k):
@@ -43,11 +44,11 @@
 
 def kernel(
     q_hbm, k_hbm, v_hbm, h_hbm, w_hbm, b_hbm,
-    att_hbm, gat_hbm,
+    final, phi_v, gat_v,
     q_v, k_v, v_v, h_v, w_v, b_v, up_v, dn_v,
     dense, state, send_c, recv_c, send_a, recv_a, send_b, recv_b, own,
-    send_z, recv_z, send_x, recv_x, send_e, recv_e, final, wide, att_v, gat_v,
-    load_sem, kv_sem, out_sem, halo_s, halo_r, c_s, c_r, a_s, a_r, b_s, b_r,
+    send_z, recv_z, send_x, recv_x, send_e, recv_e,
+    load_sem, kv_sem, halo_s, halo_r, c_s, c_r, a_s, a_r, b_s, b_r,
     z_s, z_r, x_s, x_r, e_s, e_r, g_s, g_r, f_s, f_r,
 ):
     tm = lax.axis_index("tm")
@@ -75,13 +76,12 @@
     load_h = load(h_hbm, h_v, load_sem.at[0])
     load_q = load(q_hbm, q_v, load_sem.at[1])
     load_w = load(w_hbm, w_v, load_sem.at[2])
-    load_b = load(b_hbm, b_v, load_sem.at[3])
+    load_b = load(b_hbm, b_v.at[0], load_sem.at[3])
 
     barrier = pltpu.get_barrier_semaphore()
     partners = [above, below, dev_a, dev_b] + zdev[1:] + xdev[1:]
     for device in partners:
         pl.semaphore_signal(barrier, inc=1, device_id=device, device_id_type=MESH)
-    pl.semaphore_wait(barrier, len(partners))
 
     def remote(src, dst, ss, rs, device):
         return pltpu.make_async_remote_copy(
@@ -104,15 +104,16 @@
         for copy in copies:
             copy.start()
 
-    for k in range(NP):
-        start(halos[k])
-
     lane = lax.broadcasted_iota(jnp.int32, (HDIM, 2 * HDIM), 1)
     sends = []
     core = []
     for f in range(2):
         kv[f][0].wait()
         kv[f][1].wait()
+        if f == 0:
+            pl.semaphore_wait(barrier, len(partners))
+            start(halos[0])
+            start(halos[1])
         phi = features(k_v[f].reshape(TOK, WIDTH))
         val = v_v[f].reshape(TOK, WIDTH)
         dense[:, LPAD - 128:] = jnp.zeros((HDIM, 128), jnp.float32)
@@ -216,7 +217,10 @@
         step_b.append(copy)
         q = quarter(y)
         own[f] = state[f, c, q] + recv_c[f, q].astype(jnp.float32) + recv_a[f, 0].astype(jnp.float32)
-    conv(1)
+    load_q.wait()
+    for f in range(2):
+        for r in range(2):
+            phi_v[f, r] = features(q_v[f, r])
     for f in range(2):
         step_b[f].wait_recv()
         own[f] = own[f] + recv_b[f].astype(jnp.float32)
@@ -228,7 +232,9 @@
         copy.start()
         step_z.append(copy)
     recv_z[z] = send_z[z]
-    conv(2)
+    for k in range(2, NP):
+        start(halos[k])
+    conv(1)
     for copy in step_z:
         copy.wait_recv()
     send_x[...] = sum(recv_z[j].astype(jnp.float32) for j in range(8)).astype(jnp.bfloat16)
@@ -238,7 +244,7 @@
         copy.start()
         step_x.append(copy)
     recv_x[x] = jnp.zeros((SL, 128), jnp.bfloat16)
-    conv(3)
+    conv(2)
     for copy in step_x:
         copy.wait_recv()
     running = jnp.zeros((SL, 128), jnp.float32)
@@ -253,8 +259,7 @@
         copy.start()
         step_e.append(copy)
     recv_e[z] = send_e[z]
-    load_q.wait()
-    conv(4)
+    conv(3)
     for copy in step_e:
         copy.wait_recv()
 
@@ -287,7 +292,7 @@
         step_g[f][0].wait_recv()
         step_g[f].append(spread(f, second, dev1, g_s.at[f, 2], g_r.at[f, 2]))
         forward(f, second)
-    conv(5)
+    conv(4)
     for f in range(2):
         first, dev1, second, dev2 = hops[f]
         step_g[f][1].wait_recv()
@@ -295,22 +300,31 @@
     for f in range(2):
         step_g[f][2].wait_recv()
         forward(f, opp)
-    out_g = load(gat_v, gat_hbm, out_sem.at[0])
-
+    conv(5)
+
+    for f in range(2):
+        for copy in forwards[f]:
+            copy.wait_recv()
+    for copies in halos + [core, step_a, step_b, step_z, step_x, step_e] + step_g + forwards:
+        for copy in copies:
+            copy.wait_send()
+
+
+def attend(phi_v, state_in, gat_v, att_out, gat_out, wide, att_v, sem):
+    copy_g = pltpu.make_async_copy(gat_v, gat_out, sem.at[0])
+    copy_g.start()
     same = (lax.broadcasted_iota(jnp.int32, (2 * HDIM, 2 * HDIM), 0) < HDIM) == (
         lax.broadcasted_iota(jnp.int32, (2 * HDIM, 2 * HDIM), 1) < HDIM
     )
     ones = jnp.where(same, 1.0, 0.0).astype(jnp.bfloat16)
-    out_a = []
-    for f in range(2):
-        for copy in forwards[f]:
-            copy.wait_recv()
+    outs = []
+    for f in range(2):
         for l in range(LT):
             half, at = l // HT, l % HT
-            wide[:, l * 128:(l + 1) * 128] = final[f, half, at * HDIM:(at + 1) * HDIM]
-        tails = [final[f, half, TOTROW:].astype(jnp.float32) for half in range(2)]
+            wide[:, l * 128:(l + 1) * 128] = state_in[f, half, at * HDIM:(at + 1) * HDIM]
+        tails = [state_in[f, half, TOTROW:].astype(jnp.float32) for half in range(2)]
         total = jnp.concatenate([tails[l // HT][l % HT:l % HT + 1] for l in range(LT)], axis=1)[:, :WIDTH]
-        phi = features(q_v[f].reshape(TOK, WIDTH))
+        phi = phi_v[f].reshape(TOK, WIDTH)
         scaled = (phi.astype(jnp.float32) * total).astype(jnp.bfloat16)
         for p in range(HEADS // 2):
             lo = 2 * HDIM * p
@@ -320,28 +334,25 @@
             num = jnp.dot(phi[:, lo:lo + 2 * HDIM], block, preferred_element_type=jnp.float32)
             den = jnp.dot(scaled[:, lo:lo + 2 * HDIM], ones, preferred_element_type=jnp.float32)
             att_v[f, :, :, lo:lo + 2 * HDIM] = (num / den).reshape(2, COLS, 2 * HDIM)
-        out_a.append(load(att_v.at[f], att_hbm.at[f], out_sem.at[1 + f]))
-
-    for copies in halos + [core, step_a, step_b, step_z, step_x, step_e] + step_g + forwards:
-        for copy in copies:
-            copy.wait_send()
-    out_g.wait()
-    for copy in out_a:
+        copy = pltpu.make_async_copy(att_v.at[f], att_out.at[f], sem.at[1 + f])
+        copy.start()
+        outs.append(copy)
+    copy_g.wait()
+    for copy in outs:
         copy.wait()
 
 
 def on_device(queries, key_rows, value_rows, hidden, conv_weight, conv_bias):
     bf, f32 = jnp.bfloat16, jnp.float32
     vmem, dma = pltpu.VMEM, pltpu.SemaphoreType.DMA
-    hbm = pl.BlockSpec(memory_space=pl.ANY)
-    return pl.pallas_call(
+    hbm = pl.BlockSpec(memory_space=pltpu.HBM)
+    states, phi, gated = pl.pallas_call(
         kernel,
         out_shape=(
-            jax.ShapeDtypeStruct((2, 2, COLS, WIDTH), f32),
-            jax.ShapeDtypeStruct((2, 2, COLS, HALF), bf),
+            vmem((2, 2, BLK, 128), bf), vmem((2, 2, COLS, WIDTH), bf), vmem((2, 2, COLS, HALF), bf),
         ),
         in_specs=[hbm] * 6,
-        out_specs=(hbm, hbm),
+        out_specs=(pl.BlockSpec(memory_space=pltpu.VMEM),) * 3,
         scratch_shapes=[
             vmem((2, 2, COLS, WIDTH), bf), vmem((2, 2, COLS, WIDTH), bf), vmem((2, 2, COLS, WIDTH), bf),
             vmem((2, 2, COLS, FULL), bf), vmem((3, 3, FULL), f32), vmem((1, FULL), f32),
@@ -353,18 +364,30 @@
             vmem((8, SL, 128), bf), vmem((8, SL, 128), bf),
             vmem((SL, 128), bf), vmem((4, SL, 128), bf),
             vmem((8, SL, 128), bf), vmem((8, SL, 128), bf),
-            vmem((2, 2, BLK, 128), bf), vmem((HDIM, LPAD), bf),
-            vmem((2, 2, COLS, WIDTH), f32), vmem((2, 2, COLS, HALF), bf),
-            dma((4,)), dma((2, 2)), dma((3,)), dma((NP, 2, 2)), dma((NP, 2, 2)),
+            dma((4,)), dma((2, 2)), dma((NP, 2, 2)), dma((NP, 2, 2)),
             dma((2,)), dma((2,)), dma((2,)), dma((2,)), dma((2,)), dma((2,)),
             dma((7,)), dma((7,)), dma((3,)), dma((3,)), dma((7,)), dma((7,)),
             dma((2, 3)), dma((2, 3)), dma((2, 4)), dma((2, 4)),
         ],
         compiler_params=pltpu.CompilerParams(
-            collective_id=0, has_side_effects=True, vmem_limit_bytes=48 * 1024 * 1024
+            collective_id=0, has_side_effects=True, vmem_limit_bytes=VMEM_BYTES
         ),
-        name="linear_attention_conv",
-    )(queries, key_rows, value_rows, hidden, conv_weight, conv_bias.reshape(1, FULL))
+        name="states_and_conv",
+    )(queries, key_rows, value_rows, hidden, conv_weight, conv_bias)
+    return pl.pallas_call(
+        attend,
+        out_shape=(
+            jax.ShapeDtypeStruct((2, 2, COLS, WIDTH), f32),
+            jax.ShapeDtypeStruct((2, 2, COLS, HALF), bf),
+        ),
+        in_specs=[pl.BlockSpec(memory_space=pltpu.VMEM)] * 3,
+        out_specs=(hbm, hbm),
+        scratch_shapes=[
+            vmem((HDIM, LPAD), bf), vmem((2, 2, COLS, WIDTH), f32), dma((3,)),
+        ],
+        compiler_params=pltpu.CompilerParams(vmem_limit_bytes=VMEM_BYTES),
+        name="attend",
+    )(*[pltpu.with_memory_space_constraint(a, pltpu.VMEM) for a in (phi, states, gated)])
 
 
 def solution(mesh):

time: 78.7 us -> 57 us (0.72)
  local copies, waits for them, and re-layouts: 10.9 us -> 0 us
  Pallas kernels: 66.8 us -> 56.3 us
    pallas_call x1 -> x2, Pallas kernels: 66.8 us -> 56.3 us  [the longest x1 51.5 us: on_device(): pl.pallas_call(kernel, out_shape=(vmem((2, 2, BLK, 128), bf), vmem((2, 2,...]
    unnamed x12 -> x0, local copies, waits for them, and re-layouts: 10.1 us -> none
where the time goes in v2:
time: 57 us; the launch traced here: 56.9 us
  Pallas kernels  56.3 us (99%)
  between operations  0.64 us (1%)
    pallas_call x1, Pallas kernels, on_device(): pl.pallas_call(kernel, out_shape=(vmem((2, 2, BLK, 128), bf), vmem((2, 2,...  51.5 us
    pallas_call x1, Pallas kernels, on_device(): pl.pallas_call(attend, out_shape=(jax.ShapeDtypeStruct((2, 2, COLS, WIDTH...  4.73 us

profile of v2, /device:TPU:1, one launch (start us, length us, event | category | flops | bytes accessed | tf_op | source)
XLA Modules:
  0.0 56.9 jit_solution(4636529783824950504)
XLA Ops:
  0.6 51.5 %states_and_conv.1 = (bf16[2,2,1024,128]{3,2,1,0:T(8,128)(2,1)S(1)}, bf16[2,2,80,2240]{3,2,1,0:T(8,128)(2,1)S(1)}, bf16[2,2,80,2800]{3,2,1,0:T(8,128)(2,1)S(1)}) custom-call(bf16[2,2,80,2240]{3,2,1,0:T(8,128)(2,1)} %q_hbm.1, bf16[2,2,80,2240]{3,2,1,0:T(8,128)(2,1)} %k_hbm.1, bf16[2,2,80,2240]{3,2,1,0:T(8,128)(2,1)} %v_hbm.1, bf16[2,2,80,5600]{3,2,1,0:T(8,128)(2,1)} %h_hbm.1, ...), custom_call_target="tpu_custom_call" | custom-call | tf_op jit(solution)/shard_map/states_and_conv/pallas_call | solution.py:349
  52.2 4.7 %attend.1 = (f32[2,2,80,2240]{3,2,1,0:T(8,128)}, bf16[2,2,80,2800]{3,2,1,0:T(8,128)(2,1)}) custom-call(bf16[2,2,80,2240]{3,2,1,0:T(8,128)(2,1)S(1)} %get-tuple-element.5.phi_v, bf16[2,2,1024,128]{3,2,1,0:T(8,128)(2,1)S(1)} %get-tuple-element.6.state_in, bf16[2,2,80,2800]{3,2,1,0:T(8,128)(2,1)S(1)} %get-tuple-element.7.gat_v), custom_call_target="tpu_custom_call" | custom-call | tf_op jit(solution)/shard_map/attend/pallas_call | solution.py:377

commit v3 on v2

v3 whole, which is shorter than its diff:
```python
import jax
import jax.numpy as jnp
from jax import lax
from jax.experimental import pallas as pl
from jax.experimental.pallas import tpu as pltpu
from jax.sharding import PartitionSpec as P

HEADS = 20
HDIM = 112
WIDTH = HEADS * HDIM
HALF = 2800
FULL = 2 * HALF
COLS = 80
TOK = 2 * COLS
LT = 18
LPAD = LT * 128
HT = LT // 2
BLK = 1024
TOTROW = HT * HDIM
QTR = BLK // 4
SL = QTR // 8
MESH = pl.DeviceIdType.MESH
CUTS = (0, 4, 8, 12, 16, 19, 22)
NP = len(CUTS) - 1
VMEM_BYTES = 56 * 1024 * 1024


def val_lanes(k):
    lo, hi = CUTS[k], min(CUTS[k + 1], 21)
    return lo * 128, (hi - lo) * 128


def gate_lanes(k):
    lo = 21 if k == 0 else 22 + CUTS[k]
    hi = min(22 + CUTS[k + 1], 44)
    start, end = lo * 128, min(hi * 128, FULL)
    return start, end - start


def features(x):
    x = x.astype(jnp.float32)
    return jnp.where(x > 0, x + 1.0, jnp.exp(x)).astype(jnp.bfloat16)


def kernel(
    q_hbm, k_hbm, v_hbm, h_hbm, w_hbm, b_hbm,
    final, phi_v, gat_v,
    q_v, k_v, v_v, h_v, w_v, b_v, up_v, dn_v,
    turned, state, send_c, recv_c, send_a, recv_a, own,
    send_z, recv_z, send_x, recv_x, send_e, recv_e,
    load_sem, kv_sem, halo_s, halo_r, c_s, c_r, a_s, a_r,
    z_s, z_r, x_s, x_r, e_s, e_r, g_s, g_r, f_s, f_r,
):
    tm = lax.axis_index("tm")
    row = lax.axis_index("rows")
    x, z = tm // 8, tm % 8
    y, c = row // 2, row % 2
    sib = (tm, row + 1 - 2 * c)
    above, below = (tm, (row + 7) % 8), (tm, (row + 1) % 8)
    ydev = [(tm, (y + d) % 4 * 2 + c) for d in range(4)]
    zdev = [(x * 8 + (z + d) % 8, row) for d in range(8)]
    xdev = [(((x + d) % 4) * 8 + z, row) for d in range(4)]

    def load(src, dst, sem):
        copy = pltpu.make_async_copy(src, dst, sem)
        copy.start()
        return copy

    kv = [
        (load(k_hbm.at[f], k_v.at[f], kv_sem.at[f, 0]), load(v_hbm.at[f], v_v.at[f], kv_sem.at[f, 1]))
        for f in range(2)
    ]
    load_h = load(h_hbm, h_v, load_sem.at[0])
    load_q = load(q_hbm, q_v, load_sem.at[1])
    load_w = load(w_hbm, w_v, load_sem.at[2])
    load_b = load(b_hbm, b_v.at[0], load_sem.at[3])

    barrier = pltpu.get_barrier_semaphore()
    partners = [above, below] + ydev[1:] + zdev[1:] + xdev[1:]
    for device in partners:
        pl.semaphore_signal(barrier, inc=1, device_id=device, device_id_type=MESH)

    def remote(src, dst, ss, rs, device):
        return pltpu.make_async_remote_copy(
            src_ref=src, dst_ref=dst, send_sem=ss, recv_sem=rs, device_id=device, device_id_type=MESH
        )

    def halo(k):
        copies = []
        for n, (start, size) in enumerate((val_lanes(k), gate_lanes(k))):
            lanes = pl.ds(start, size)
            copies.append(remote(h_hbm.at[:, 1, :, lanes], up_v.at[:, :, lanes],
                                 halo_s.at[k, n, 0], halo_r.at[k, n, 0], below))
            copies.append(remote(h_hbm.at[:, 0, :, lanes], dn_v.at[:, :, lanes],
                                 halo_s.at[k, n, 1], halo_r.at[k, n, 1], above))
        return copies

    halos = [halo(k) for k in range(NP)]

    def start(copies):
        for copy in copies:
            copy.start()

    core = []
    for f in range(2):
        kv[f][0].wait()
        sums = []
        for l in range(LT):
            n = min(128, WIDTH - 128 * l)
            phi = features(k_v[f, :, :, 128 * l:128 * l + n].reshape(TOK, n))
            turned[128 * l:128 * l + n] = phi.T
            sums.append(jnp.sum(phi.astype(jnp.float32), axis=0, keepdims=True))
        sums[-1] = jnp.concatenate([sums[-1], jnp.zeros((1, LPAD - WIDTH), jnp.float32)], axis=1)
        for half in range(2):
            rows = sums[half * HT:(half + 1) * HT] + [jnp.zeros((BLK - TOTROW - HT, 128), jnp.float32)]
            part = jnp.concatenate(rows, axis=0)
            state[f, half, TOTROW:] = part if f == 0 else part + state[0, half, TOTROW:]
        kv[f][1].wait()
        for m in range(HT):
            c0, c1 = 256 * m, min(256 * (m + 1), WIDTH)
            h0, h1 = c0 // HDIM, -(-c1 // HDIM)
            val = v_v[f, :, :, c0:c1].reshape(TOK, c1 - c0)
            prod = jnp.dot(turned[HDIM * h0:HDIM * h1], val, preferred_element_type=jnp.float32)
            for l in range(c0 // 128, -(-c1 // 128)):
                l0, l1 = 128 * l, min(128 * (l + 1), WIDTH)
                head = l0 // HDIM
                at = HDIM * (head - h0)
                part = prod[at:at + HDIM, l0 - c0:l1 - c0]
                if HDIM * (head + 1) < l1:
                    lane = lax.broadcasted_iota(jnp.int32, part.shape, 1)
                    part = jnp.where(lane < HDIM * (head + 1) - l0, part, prod[at + HDIM:at + 2 * HDIM, l0 - c0:l1 - c0])
                if l1 - l0 < 128:
                    part = jnp.concatenate([part, jnp.zeros((HDIM, 128 - l1 + l0), jnp.float32)], axis=1)
                half, rows = l // HT, slice(l % HT * HDIM, (l % HT + 1) * HDIM)
                state[f, half, rows] = part if f == 0 else part + state[0, half, rows]
        if f == 0:
            pl.semaphore_wait(barrier, len(partners))
            start(halos[0])
            start(halos[1])
        send_c[f] = state[f, 1 - c].astype(jnp.bfloat16)
        copy = remote(send_c.at[f], recv_c.at[f], c_s.at[f], c_r.at[f], sib)
        copy.start()
        core.append(copy)

    load_h.wait()
    load_w.wait()
    load_b.wait()
    top = jnp.where(row > 0, 1.0, 0.0)
    bottom = jnp.where(row < 7, 1.0, 0.0)
    shift = FULL - HALF - 22 * 128 + 128
    col8 = lax.broadcasted_iota(jnp.int32, (8, 128), 0)

    def place(size, n):
        at, to = lax.broadcasted_iota(jnp.int32, (size, n), 0), lax.broadcasted_iota(jnp.int32, (size, n), 1)
        return jnp.where(at == to + shift, 1.0, 0.0).astype(jnp.bfloat16)

    def conv_tile(rows, bias, weight):
        first, last = [weight[0] * top, weight[1], weight[2]], [weight[0], weight[1], weight[2] * bottom]
        edge = col8[:, :bias.shape[1]]
        outs = []
        for o, weights in ((0, first), (1, last)):
            parts = []
            for j in range(3):
                parts.append(sum(rows[o + i] * weights[i][j:j + 1] for i in range(3)))
            left = jnp.concatenate([parts[0][:72], jnp.where(edge < 7, parts[0][72:], 0.0)], axis=0)
            right = jnp.concatenate([jnp.where(edge > 0, parts[2][:8], 0.0), parts[2][8:]], axis=0)
            outs.append(parts[1] + bias + pltpu.roll(left, 1, 0) + pltpu.roll(right, COLS - 1, 0))
        return outs

    def input_rows(f, src):
        return [up_v[f, :, src], h_v[f, 0, :, src], h_v[f, 1, :, src], dn_v[f, :, src]]

    def conv_out(a, n):
        gate_at = (21 + a) * 128
        if n == 128:
            size = 256
            gate_src = pl.ds(pl.multiple_of(gate_at, 128), size)
            value_src = pl.ds(pl.multiple_of(a * 128, 128), 128)
        else:
            size = FULL - gate_at
            gate_src = pl.ds(gate_at, size)
            value_src = pl.ds(a * 128, 128)
        move = place(size, n)
        gates = []
        for f in range(2):
            rows = jnp.concatenate(input_rows(f, gate_src), axis=0)
            rows = jnp.dot(rows, move, preferred_element_type=jnp.float32)
            gates.append(conv_tile(
                [rows[i * COLS:(i + 1) * COLS] for i in range(4)],
                b_v[:, gate_src][:, shift:shift + n], [w_v[i, :, gate_src][:, shift:shift + n] for i in range(3)],
            ))
        for f in range(2):
            value = conv_tile(
                [r[:, :n].astype(jnp.float32) for r in input_rows(f, value_src)],
                b_v[:, value_src][:, :n], [w_v[i, :, value_src][:, :n] for i in range(3)],
            )
            for o in range(2):
                part = 0.5 * gates[f][o]
                gated = value[o] * (part + part * jnp.tanh(part))
                gat_v[f, o, :, pl.ds(a * 128 if n < 128 else pl.multiple_of(a * 128, 128), n)] = gated.astype(jnp.bfloat16)

    def conv(k):
        for copy in halos[k]:
            copy.wait_recv()
        if 0 < k < NP - 2:
            start(halos[k + 2])
        lo, hi = CUTS[k], min(CUTS[k + 1], 21)

        @pl.loop(lo, hi)
        def _(a):
            conv_out(a, 128)

        if CUTS[k + 1] == 22:
            conv_out(21, HALF - 21 * 128)

    def quarter(q):
        return pl.ds(pl.multiple_of(q * QTR, QTR), QTR)

    load_q.wait()
    for f in range(2):
        for r in range(2):
            phi_v[f, r] = features(q_v[f, r])

    step_a = [[], []]

    def scatter(f):
        core[f].wait_recv()
        full = state[f, c] + recv_c[f].astype(jnp.float32)
        state[f, c] = full
        send_a[f] = full.astype(jnp.bfloat16).reshape(4, QTR, 128)
        for d in (2, 1, 3):
            copy = remote(send_a.at[f, (y + d) % 4], recv_a.at[f, d - 1], a_s.at[f, d - 1], a_r.at[f, d - 1], ydev[d])
            copy.start()
            step_a[f].append(copy)

    def gather(f):
        for copy in step_a[f]:
            copy.wait_recv()
        own[f] = state[f, c, quarter(y)] + sum(recv_a[f, d].astype(jnp.float32) for d in range(3))

    scatter(1)
    start(halos[2])
    conv(0)
    conv(1)
    gather(1)

    send_z[...] = own[1].astype(jnp.bfloat16).reshape(8, SL, 128)
    step_z = []
    for d in (4, 3, 5, 2, 6, 1, 7):
        copy = remote(send_z.at[(z + d) % 8], recv_z.at[z], z_s.at[d - 1], z_r.at[d - 1], zdev[d])
        copy.start()
        step_z.append(copy)
    recv_z[z] = send_z[z]
    scatter(0)
    for copy in step_z:
        copy.wait_recv()
    send_x[...] = sum(recv_z[j].astype(jnp.float32) for j in range(8)).astype(jnp.bfloat16)
    step_x = []
    for d in (2, 1, 3):
        copy = remote(send_x, recv_x.at[x], x_s.at[d - 1], x_r.at[d - 1], xdev[d])
        copy.start()
        step_x.append(copy)
    recv_x[x] = jnp.zeros((SL, 128), jnp.bfloat16)
    conv(2)
    for copy in step_x:
        copy.wait_recv()
    running = jnp.zeros((SL, 128), jnp.float32)
    for i in range(4):
        running = running + jnp.where(i < x, recv_x[i].astype(jnp.float32), 0.0)
    for j in range(8):
        send_e[j] = running.astype(jnp.bfloat16)
        running = running + recv_z[j].astype(jnp.float32)
    step_e = []
    for d in (4, 3, 5, 2, 6, 1, 7):
        copy = remote(send_e.at[(z + d) % 8], recv_e.at[z], e_s.at[d - 1], e_r.at[d - 1], zdev[d])
        copy.start()
        step_e.append(copy)
    recv_e[z] = send_e[z]
    conv(3)
    gather(0)
    for copy in step_e:
        copy.wait_recv()

    before = recv_e[...].reshape(QTR, 128).astype(jnp.float32)
    for f in range(2):
        final[c, y, f] = (before + own[f]).astype(jnp.bfloat16)

    step_g, forwards = [], []

    def spread(q, dev, ss, rs):
        ref = final.at[c, q]
        copy = remote(ref, ref, ss, rs, dev)
        copy.start()
        return copy

    for d in (2, 1, 3):
        step_g.append(spread(y, ydev[d], g_s.at[d - 1], g_r.at[d - 1]))
    forwards.append(spread(y, sib, f_s.at[0], f_r.at[0]))
    conv(4)
    for n, d in ((1, 1), (2, 3), (0, 2)):
        step_g[n].wait_recv()
        forwards.append(spread((y + 4 - d) % 4, sib, f_s.at[d], f_r.at[d]))
    conv(5)
    for copy in forwards:
        copy.wait_recv()
    for copies in halos + step_a + [core, step_z, step_x, step_e, step_g, forwards]:
        for copy in copies:
            copy.wait_send()


def attend(phi_v, state_in, gat_v, att_out, gat_out, scaled, att_v, sem):
    copy_g = pltpu.make_async_copy(gat_v, gat_out, sem.at[0])
    copy_g.start()
    bf, f32 = jnp.bfloat16, jnp.float32
    for f in range(2):
        tails = [state_in[half, 3, f, TOTROW - 3 * QTR:].astype(f32) for half in range(2)]
        total = jnp.concatenate([tails[l // HT][l % HT:l % HT + 1] for l in range(LT)], axis=1)[:, :WIDTH]
        scaled[f] = (phi_v[f].reshape(TOK, WIDTH).astype(f32) * total).astype(bf)

    def state_tile(f, l):
        at, end, parts = l % HT * HDIM, (l % HT + 1) * HDIM, []
        while at < end:
            q, row = at // QTR, at % QTR
            n = min(end - at, QTR - row)
            parts.append(state_in[l // HT, q, f, row:row + n])
            at += n
        return jnp.concatenate(parts, axis=0)

    outs, done = [copy_g], 0
    for m in range(HT):
        c0, c1 = 256 * m, min(256 * (m + 1), WIDTH)
        h0, h1 = c0 // HDIM, -(-c1 // HDIM)
        w0, w1 = HDIM * h0 // 128 * 128, min(-(-HDIM * h1 // 128) * 128, WIDTH)
        lane = lax.broadcasted_iota(jnp.int32, (HDIM, c1 - c0), 1)
        masks = [(lane >= HDIM * h - c0) & (lane < HDIM * (h + 1) - c0) for h in range(h0, h1)]

        def stack(parts):
            before, after = HDIM * h0 - w0, w1 - HDIM * h1
            if before:
                parts = [jnp.zeros((before, c1 - c0), bf)] + parts
            if after:
                parts = parts + [jnp.zeros((after, c1 - c0), bf)]
            return jnp.concatenate(parts, axis=0)

        ones = stack([jnp.where(mask, 1.0, 0.0).astype(bf) for mask in masks])
        for f in range(2):
            block = jnp.concatenate([state_tile(f, l) for l in range(c0 // 128, -(-c1 // 128))], axis=1)[:, :c1 - c0]
            block = stack([jnp.where(mask, block, jnp.zeros_like(block)) for mask in masks])
            num = jnp.dot(phi_v[f, :, :, w0:w1].reshape(TOK, w1 - w0), block, preferred_element_type=f32)
            den = jnp.dot(scaled[f, :, w0:w1], ones, preferred_element_type=f32)
            att_v[f, :, :, c0:c1] = (num / den).reshape(2, COLS, c1 - c0)
        if m in (1, 3, 5, 7, 8):
            lanes = pl.ds(done, c1 - done)
            copy = pltpu.make_async_copy(att_v.at[:, :, :, lanes], att_out.at[:, :, :, lanes], sem.at[len(outs)])
            copy.start()
            outs.append(copy)
            done = c1
    for copy in outs:
        copy.wait()


def on_device(queries, key_rows, value_rows, hidden, conv_weight, conv_bias):
    bf, f32 = jnp.bfloat16, jnp.float32
    vmem, dma = pltpu.VMEM, pltpu.SemaphoreType.DMA
    hbm = pl.BlockSpec(memory_space=pltpu.HBM)
    states, phi, gated = pl.pallas_call(
        kernel,
        out_shape=(
            vmem((2, 4, 2, QTR, 128), bf), vmem((2, 2, COLS, WIDTH), bf), vmem((2, 2, COLS, HALF), bf),
        ),
        in_specs=[hbm] * 6,
        out_specs=(pl.BlockSpec(memory_space=pltpu.VMEM),) * 3,
        scratch_shapes=[
            vmem((2, 2, COLS, WIDTH), bf), vmem((2, 2, COLS, WIDTH), bf), vmem((2, 2, COLS, WIDTH), bf),
            vmem((2, 2, COLS, FULL), bf), vmem((3, 3, FULL), f32), vmem((1, FULL), f32),
            vmem((2, COLS, FULL), bf), vmem((2, COLS, FULL), bf),
            vmem((WIDTH, TOK), bf), vmem((2, 2, BLK, 128), f32),
            vmem((2, BLK, 128), bf), vmem((2, BLK, 128), bf),
            vmem((2, 4, QTR, 128), bf), vmem((2, 3, QTR, 128), bf), vmem((2, QTR, 128), f32),
            vmem((8, SL, 128), bf), vmem((8, SL, 128), bf),
            vmem((SL, 128), bf), vmem((4, SL, 128), bf),
            vmem((8, SL, 128), bf), vmem((8, SL, 128), bf),
            dma((4,)), dma((2, 2)), dma((NP, 2, 2)), dma((NP, 2, 2)),
            dma((2,)), dma((2,)), dma((2, 3)), dma((2, 3)),
            dma((7,)), dma((7,)), dma((3,)), dma((3,)), dma((7,)), dma((7,)),
            dma((3,)), dma((3,)), dma((4,)), dma((4,)),
        ],
        compiler_params=pltpu.CompilerParams(
            collective_id=0, has_side_effects=True, vmem_limit_bytes=VMEM_BYTES
        ),
        name="states_and_conv",
    )(queries, key_rows, value_rows, hidden, conv_weight, conv_bias)
    return pl.pallas_call(
        attend,
        out_shape=(
            jax.ShapeDtypeStruct((2, 2, COLS, WIDTH), f32),
            jax.ShapeDtypeStruct((2, 2, COLS, HALF), bf),
        ),
        in_specs=[pl.BlockSpec(memory_space=pltpu.VMEM)] * 3,
        out_specs=(hbm, hbm),
        scratch_shapes=[
            vmem((2, TOK, WIDTH), bf), vmem((2, 2, COLS, WIDTH), f32), dma((6,)),
        ],
        compiler_params=pltpu.CompilerParams(vmem_limit_bytes=VMEM_BYTES),
        name="attend",
    )(*[pltpu.with_memory_space_constraint(a, pltpu.VMEM) for a in (phi, states, gated)])


def solution(mesh):
    block = P("tm", "rows", None, None)
    return jax.shard_map(
        on_device, mesh=mesh, in_specs=(block, block, block, block, P(), P()),
        out_specs=(block, block), check_vma=False,
    )
```

time: 57 us -> 48.8 us (0.86)
  Pallas kernels: 56.3 us -> 48.1 us
    pallas_call x1, Pallas kernels: 51.5 us -> 45.5 us  [on_device(): pl.pallas_call(kernel, out_shape=(vmem((2, 4, 2, QTR, 128), bf), vmem((2,...]
    pallas_call x1, Pallas kernels: 4.73 us -> 2.55 us  [on_device(): pl.pallas_call(attend, out_shape=(jax.ShapeDtypeStruct((2, 2, COLS, WIDTH...]
where the time goes in v3:
time: 48.8 us; the launch traced here: 48.7 us
  Pallas kernels  48.1 us (99%)
  between operations  0.64 us (1%)
    pallas_call x1, Pallas kernels, on_device(): pl.pallas_call(kernel, out_shape=(vmem((2, 4, 2, QTR, 128), bf), vmem((2,...  45.5 us
    pallas_call x1, Pallas kernels, on_device(): pl.pallas_call(attend, out_shape=(jax.ShapeDtypeStruct((2, 2, COLS, WIDTH...  2.55 us

profile of v3, /device:TPU:1, one launch (start us, length us, event | category | flops | bytes accessed | tf_op | source)
XLA Modules:
  0.0 48.7 jit_solution(16109635276959483248)
XLA Ops:
  0.6 45.5 %states_and_conv.1 = (bf16[2,4,2,256,128]{4,3,2,1,0:T(8,128)(2,1)S(1)}, bf16[2,2,80,2240]{3,2,1,0:T(8,128)(2,1)S(1)}, bf16[2,2,80,2800]{3,2,1,0:T(8,128)(2,1)S(1)}) custom-call(bf16[2,2,80,2240]{3,2,1,0:T(8,128)(2,1)} %q_hbm.1, bf16[2,2,80,2240]{3,2,1,0:T(8,128)(2,1)} %k_hbm.1, bf16[2,2,80,2240]{3,2,1,0:T(8,128)(2,1)} %v_hbm.1, ...), custom_call_target="tpu_custom_call" | custom-call | tf_op jit(solution)/shard_map/states_and_conv/pallas_call | solution.py:366
  46.2 2.5 %attend.1 = (f32[2,2,80,2240]{3,2,1,0:T(8,128)}, bf16[2,2,80,2800]{3,2,1,0:T(8,128)(2,1)}) custom-call(bf16[2,2,80,2240]{3,2,1,0:T(8,128)(2,1)S(1)} %get-tuple-element.5.phi_v, bf16[2,4,2,256,128]{4,3,2,1,0:T(8,128)(2,1)S(1)} %get-tuple-element.6.state_in, bf16[2,2,80,2800]{3,2,1,0:T(8,128)(2,1)S(1)} %get-tuple-element.7.gat_v), custom_call_target="tpu_custom_call" | custom-call | tf_op jit(solution)/shard_map/attend/pallas_call | solution.py:393

commit v4 on v3

--- a/solution.py
+++ b/solution.py
@@ -20,7 +20,7 @@
 QTR = BLK // 4
 SL = QTR // 8
 MESH = pl.DeviceIdType.MESH
-CUTS = (0, 4, 8, 12, 16, 19, 22)
+CUTS = (0, 4, 8, 12, 16, 20, 22)
 NP = len(CUTS) - 1
 VMEM_BYTES = 56 * 1024 * 1024
 
@@ -100,6 +100,9 @@
     def start(copies):
         for copy in copies:
             copy.start()
+
+    pl.semaphore_wait(barrier, len(partners))
+    start(halos[0])
 
     core = []
     for f in range(2):
@@ -133,10 +136,6 @@
                     part = jnp.concatenate([part, jnp.zeros((HDIM, 128 - l1 + l0), jnp.float32)], axis=1)
                 half, rows = l // HT, slice(l % HT * HDIM, (l % HT + 1) * HDIM)
                 state[f, half, rows] = part if f == 0 else part + state[0, half, rows]
-        if f == 0:
-            pl.semaphore_wait(barrier, len(partners))
-            start(halos[0])
-            start(halos[1])
         send_c[f] = state[f, 1 - c].astype(jnp.bfloat16)
         copy = remote(send_c.at[f], recv_c.at[f], c_s.at[f], c_r.at[f], sib)
         copy.start()
@@ -202,8 +201,6 @@
     def conv(k):
         for copy in halos[k]:
             copy.wait_recv()
-        if 0 < k < NP - 2:
-            start(halos[k + 2])
         lo, hi = CUTS[k], min(CUTS[k + 1], 21)
 
         @pl.loop(lo, hi)
@@ -239,9 +236,9 @@
         own[f] = state[f, c, quarter(y)] + sum(recv_a[f, d].astype(jnp.float32) for d in range(3))
 
     scatter(1)
+    start(halos[1])
     start(halos[2])
     conv(0)
-    conv(1)
     gather(1)
 
     send_z[...] = own[1].astype(jnp.bfloat16).reshape(8, SL, 128)
@@ -252,6 +249,8 @@
         step_z.append(copy)
     recv_z[z] = send_z[z]
     scatter(0)
+    start(halos[3])
+    conv(1)
     for copy in step_z:
         copy.wait_recv()
     send_x[...] = sum(recv_z[j].astype(jnp.float32) for j in range(8)).astype(jnp.bfloat16)
@@ -261,7 +260,7 @@
         copy.start()
         step_x.append(copy)
     recv_x[x] = jnp.zeros((SL, 128), jnp.bfloat16)
-    conv(2)
+    start(halos[4])
     for copy in step_x:
         copy.wait_recv()
     running = jnp.zeros((SL, 128), jnp.float32)
@@ -276,7 +275,7 @@
         copy.start()
         step_e.append(copy)
     recv_e[z] = send_e[z]
-    conv(3)
+    conv(2)
     gather(0)
     for copy in step_e:
         copy.wait_recv()
@@ -296,6 +295,8 @@
     for d in (2, 1, 3):
         step_g.append(spread(y, ydev[d], g_s.at[d - 1], g_r.at[d - 1]))
     forwards.append(spread(y, sib, f_s.at[0], f_r.at[0]))
+    start(halos[5])
+    conv(3)
     conv(4)
     for n, d in ((1, 1), (2, 3), (0, 2)):
         step_g[n].wait_recv()

time: 48.8 us -> 48 us (0.984)
  Pallas kernels: 48.1 us -> 47.3 us
    pallas_call x1, Pallas kernels: 45.5 us -> 44.7 us  [on_device(): pl.pallas_call(kernel, out_shape=(vmem((2, 4, 2, QTR, 128), bf), vmem((2,...]
where the time goes in v4:
time: 48 us; the launch traced here: 47.9 us
  Pallas kernels  47.3 us (99%)
  between operations  0.64 us (1%)
    pallas_call x1, Pallas kernels, on_device(): pl.pallas_call(kernel, out_shape=(vmem((2, 4, 2, QTR, 128), bf), vmem((2,...  44.7 us
    pallas_call x1, Pallas kernels, on_device(): pl.pallas_call(attend, out_shape=(jax.ShapeDtypeStruct((2, 2, COLS, WIDTH...  2.55 us

profile of v4, /device:TPU:1, one launch (start us, length us, event | category | flops | bytes accessed | tf_op | source)
XLA Modules:
  0.0 47.9 jit_solution(5372791411308020082)
XLA Ops:
  0.6 44.7 %states_and_conv.1 = (bf16[2,4,2,256,128]{4,3,2,1,0:T(8,128)(2,1)S(1)}, bf16[2,2,80,2240]{3,2,1,0:T(8,128)(2,1)S(1)}, bf16[2,2,80,2800]{3,2,1,0:T(8,128)(2,1)S(1)}) custom-call(bf16[2,2,80,2240]{3,2,1,0:T(8,128)(2,1)} %q_hbm.1, bf16[2,2,80,2240]{3,2,1,0:T(8,128)(2,1)} %k_hbm.1, bf16[2,2,80,2240]{3,2,1,0:T(8,128)(2,1)} %v_hbm.1, ...), custom_call_target="tpu_custom_call" | custom-call | tf_op jit(solution)/shard_map/states_and_conv/pallas_call | solution.py:367
  45.4 2.5 %attend.1 = (f32[2,2,80,2240]{3,2,1,0:T(8,128)}, bf16[2,2,80,2800]{3,2,1,0:T(8,128)(2,1)}) custom-call(bf16[2,2,80,2240]{3,2,1,0:T(8,128)(2,1)S(1)} %get-tuple-element.5.phi_v, bf16[2,4,2,256,128]{4,3,2,1,0:T(8,128)(2,1)S(1)} %get-tuple-element.6.state_in, bf16[2,2,80,2800]{3,2,1,0:T(8,128)(2,1)S(1)} %get-tuple-element.7.gat_v), custom_call_target="tpu_custom_call" | custom-call | tf_op jit(solution)/shard_map/attend/pallas_call | solution.py:394

commit v5 on v4

--- a/solution.py
+++ b/solution.py
@@ -97,9 +97,19 @@
 
     halos = [halo(k) for k in range(NP)]
 
+    def each(copies, act):
+        @pl.when(row < 7)
+        def _():
+            for copy in copies[0::2]:
+                act(copy)
+
+        @pl.when(row > 0)
+        def _():
+            for copy in copies[1::2]:
+                act(copy)
+
     def start(copies):
-        for copy in copies:
-            copy.start()
+        each(copies, lambda copy: copy.start())
 
     pl.semaphore_wait(barrier, len(partners))
     start(halos[0])
@@ -141,6 +151,14 @@
         copy.start()
         core.append(copy)
 
+    @pl.when(row == 0)
+    def _():
+        up_v[...] = jnp.zeros_like(up_v)
+
+    @pl.when(row == 7)
+    def _():
+        dn_v[...] = jnp.zeros_like(dn_v)
+
     load_h.wait()
     load_w.wait()
     load_b.wait()
@@ -199,8 +217,16 @@
                 gat_v[f, o, :, pl.ds(a * 128 if n < 128 else pl.multiple_of(a * 128, 128), n)] = gated.astype(jnp.bfloat16)
 
     def conv(k):
-        for copy in halos[k]:
-            copy.wait_recv()
+        @pl.when(row > 0)
+        def _():
+            for copy in halos[k][0::2]:
+                copy.wait_recv()
+
+        @pl.when(row < 7)
+        def _():
+            for copy in halos[k][1::2]:
+                copy.wait_recv()
+
         lo, hi = CUTS[k], min(CUTS[k + 1], 21)
 
         @pl.loop(lo, hi)
@@ -304,7 +330,9 @@
     conv(5)
     for copy in forwards:
         copy.wait_recv()
-    for copies in halos + step_a + [core, step_z, step_x, step_e, step_g, forwards]:
+    for copies in halos:
+        each(copies, lambda copy: copy.wait_send())
+    for copies in step_a + [core, step_z, step_x, step_e, step_g, forwards]:
         for copy in copies:
             copy.wait_send()
 

time: 48 us -> 47.4 us (0.987)
  Pallas kernels: 47.3 us -> 46.7 us
    pallas_call x1, Pallas kernels: 44.7 us -> 44.2 us  [on_device(): pl.pallas_call(kernel, out_shape=(vmem((2, 4, 2, QTR, 128), bf), vmem((2,...]
where the time goes in v5:
time: 47.4 us; the launch traced here: 47.3 us
  Pallas kernels  46.7 us (99%)
  between operations  0.64 us (1%)
    pallas_call x1, Pallas kernels, on_device(): pl.pallas_call(kernel, out_shape=(vmem((2, 4, 2, QTR, 128), bf), vmem((2,...  44.2 us
    pallas_call x1, Pallas kernels, on_device(): pl.pallas_call(attend, out_shape=(jax.ShapeDtypeStruct((2, 2, COLS, WIDTH...  2.55 us

profile of v5, /device:TPU:1, one launch (start us, length us, event | category | flops | bytes accessed | tf_op | source)
XLA Modules:
  0.0 47.3 jit_solution(3333359401239045451)
XLA Ops:
  0.6 44.2 %states_and_conv.1 = (bf16[2,4,2,256,128]{4,3,2,1,0:T(8,128)(2,1)S(1)}, bf16[2,2,80,2240]{3,2,1,0:T(8,128)(2,1)S(1)}, bf16[2,2,80,2800]{3,2,1,0:T(8,128)(2,1)S(1)}) custom-call(bf16[2,2,80,2240]{3,2,1,0:T(8,128)(2,1)} %q_hbm.1, bf16[2,2,80,2240]{3,2,1,0:T(8,128)(2,1)} %k_hbm.1, bf16[2,2,80,2240]{3,2,1,0:T(8,128)(2,1)} %v_hbm.1, ...), custom_call_target="tpu_custom_call" | custom-call | tf_op jit(solution)/shard_map/states_and_conv/pallas_call | solution.py:395
  44.8 2.5 %attend.1 = (f32[2,2,80,2240]{3,2,1,0:T(8,128)}, bf16[2,2,80,2800]{3,2,1,0:T(8,128)(2,1)}) custom-call(bf16[2,2,80,2240]{3,2,1,0:T(8,128)(2,1)S(1)} %get-tuple-element.5.phi_v, bf16[2,4,2,256,128]{4,3,2,1,0:T(8,128)(2,1)S(1)} %get-tuple-element.6.state_in, bf16[2,2,80,2800]{3,2,1,0:T(8,128)(2,1)S(1)} %get-tuple-element.7.gat_v), custom_call_target="tpu_custom_call" | custom-call | tf_op jit(solution)/shard_map/attend/pallas_call | solution.py:422
